TPU v7x, 256 devices: a whole 4x4x8 slice. The times are simulated.
256 devices in a mesh: pert: 2 (over x_lo), band: 16 (over z, core), pw: 8 (over x_hi, y).
Axes of the slice: x: 4 (x_hi: 2, x_lo: 2; x = x_hi * 2 + x_lo), y: 4, z: 8, core: 2. Of those that a mesh axis runs over, the one named last changes fastest.
Arguments:
- trial_potential: float32 [2, 128, 64, 128], P(None, 'pw'), may hold values from -6 to 6
- local_potential: float32 [128, 64, 128], P('pw'), may hold values from -0.5 to 0.5
- psi_coef: float32 [131072, 16], P('pw', 'band'), may hold values from -6 to 6
- band_energy: float32 [16], replicated, may hold values from -1 to -0.4
- band_slot: int32 [16], P('band'), may hold values from 0 to 15, each once
- pw_index: int32 [131072], P('pw'), may hold values from 0 to 131071, as said below
Outputs:
- density_response: float32 [2, 128, 64, 128], P('pert', 'pw', 'band')
- intersections: float32 [2, 2], replicated
Inputs may be any that keep to these rules, and one draw needn't show every extreme that they name: `pw_index`: entry j of each aligned run of 16384 entries is a cell q * 128 + kz of the line q = (j mod 16384) // 16, with kz below 128; the kz of the 16 entries of one line are distinct. `band_slot`: each band appears in exactly one slot.
All inputs are finite; a program needn't handle non-finite values.
Results may differ from a plain program's by a relative error of at most 0.0001.
Values sent between devices are 32-bit elements; how exact they have to be, the bound alone decides.
No kernel may reach another device: no remote copies, remote signals or barrier semaphores. Data moves between devices by JAX's collectives and lax.ppermute only.
A program may use at most 192 MiB of HBM per device.

v0:
```python
import math
from functools import partial

import jax
import jax.numpy as jnp
import numpy as np
from jax import lax
from jax.experimental import pallas as pl
from jax.experimental.pallas import tpu as pltpu
from jax.sharding import PartitionSpec as P

ITERS = 3
F32 = jnp.float32
BF16 = jnp.bfloat16
GROUP = 16
VMEM_LIMIT = 16 * 1024 * 1024


def hartley_pieces(points):
    wave_index = np.arange(points)
    angles = (wave_index[:, None] * wave_index[None, :] % points) * (2.0 * math.pi / points)
    table = (np.cos(angles) + np.sin(angles)) / math.sqrt(points)
    high = table.astype(np.float32).astype(jnp.bfloat16)
    low = (table - high.astype(np.float64)).astype(np.float32).astype(jnp.bfloat16)
    return high, low


def left_table(points):
    high, low = hartley_pieces(points)
    return np.concatenate([high, high, low], axis=1)


def right_table(points):
    high, low = hartley_pieces(points)
    return np.concatenate([high, high, low], axis=0)


def stack_pieces(values, axis):
    high = values.astype(BF16)
    low = (values - high.astype(F32)).astype(BF16)
    return jnp.concatenate([high, low, high], axis=axis)


def from_left(table, values):
    return jnp.dot(table, stack_pieces(values, 0), preferred_element_type=F32)


def all_from_left(table, blocks):
    results = []
    for first in range(0, len(blocks), 2):
        pair = blocks[first : first + 2]
        width = pair[0].shape[1]
        wide = from_left(table, jnp.concatenate(pair, axis=1))
        results += [wide[:, n * width : (n + 1) * width] for n in range(len(pair))]
    return results


def from_right(values, table):
    return jnp.dot(stack_pieces(values, 1), table, preferred_element_type=F32)


def pick(values, lanes):
    return jnp.take_along_axis(values, lanes, axis=1, mode="promise_in_bounds")


def lane_numbers(shape):
    return lax.broadcasted_iota(jnp.int32, shape, len(shape) - 1)


class Sizes:
    def __init__(self, size_x, size_y, size_z, parts, per_line):
        self.x, self.y, self.z, self.parts, self.c = size_x, size_y, size_z, parts, per_line
        self.slab_x, self.slab_y = size_x // parts, size_y // parts


def send_lines(s, flat, inverse_ref, table_x, send_ref):
    placed = []
    for ky in range(s.slab_y):
        lanes = inverse_ref[ky]
        placed.append(jnp.where(lanes >= 0, pick(flat, jnp.maximum(lanes, 0)), 0.0))
    for ky, lines in enumerate(all_from_left(table_x, placed)):
        for part in range(s.parts):
            rows = lines[part * s.slab_x : (part + 1) * s.slab_x]
            send_ref[part, pl.ds(ky, s.slab_x, s.slab_y), :] = rows


def read_lines(s, recv_ref, depth, table_x):
    result = jnp.zeros((s.x, s.slab_y * s.c), F32)
    group = lane_numbers(result.shape) // s.c
    blocks = [
        jnp.concatenate(
            [
                recv_ref[source, pl.ds(ky, s.slab_x, s.slab_y), :]
                for source in range(s.parts)
            ],
            axis=0,
        )
        for ky in range(s.slab_y)
    ]
    for ky, lines in enumerate(all_from_left(table_x, blocks)):
        result = jnp.where(group == ky, pick(lines, depth), result)
    return result


def slabs_in(s, recv_ref, rows, table_y):
    blocks = [
        recv_ref[:, row * s.slab_y : (row + 1) * s.slab_y, :].reshape(s.y, s.z) for row in rows
    ]
    return jnp.concatenate(all_from_left(table_y, blocks), axis=0)


def slabs_out(s, values, table_y, send_ref, rows):
    blocks = [values[n * s.y : (n + 1) * s.y] for n in range(len(rows))]
    for row, lines in zip(rows, all_from_left(table_y, blocks)):
        start = row * s.slab_y
        send_ref[:, start : start + s.slab_y, :] = lines.reshape(s.parts, s.slab_y, s.z)


def fold(dots):
    half = dots.shape[0] // 2
    middle = dots.shape[1] // 2
    folded = dots + pltpu.roll(dots, middle, 1)
    return jnp.where(lane_numbers((half, dots.shape[1])) < middle, folded[:half], folded[half:])


def band_dots(all_bands, flat):
    sums = [
        jnp.sum(all_bands[band] * flat, axis=0, keepdims=True)
        for band in range(all_bands.shape[0])
    ]
    return jnp.concatenate(sums, axis=0)


def band_sum(all_bands, weights):
    total = weights[0:1, :] * all_bands[0]
    for band in range(1, all_bands.shape[0]):
        total = total + weights[band : band + 1, :] * all_bands[band]
    return total


def total_weights(parts, coef_total):
    summed = jnp.sum(parts, axis=0) * (1.0 / coef_total)
    early = lane_numbers(summed.shape) < summed.shape[1] // 2
    halves = [
        jnp.sum(jnp.where(early, summed, 0.0), axis=1, keepdims=True),
        jnp.sum(jnp.where(early, 0.0, summed), axis=1, keepdims=True),
    ]
    weights = jnp.concatenate(halves, axis=0)
    return jnp.broadcast_to(weights, (weights.shape[0], summed.shape[1]))


def wave_energy(wave_number, points):
    folded = jnp.minimum(wave_number, points - wave_number).astype(F32)
    return 4.0 * (folded * (1.0 / points)) ** 2


def start_kernel(s, part_ref, slot_ref, energy_any, psi_any, index_any, tx_any,
                 send_ref, inverse_ref, depth_ref, diag_ref,
                 energy_ref, psi_ref, index_ref, tx_ref, sems):
    copies = [
        pltpu.make_async_copy(source, target, sems.at[number])
        for number, (source, target) in enumerate(
            ((index_any, index_ref), (energy_any, energy_ref), (psi_any, psi_ref), (tx_any, tx_ref))
        )
    ]
    for copy in copies:
        copy.start()
    for copy in copies:
        copy.wait()
    depth = index_ref[...] % s.z
    depth_ref[...] = depth
    turned = depth.T
    cells = lax.broadcasted_iota(jnp.int32, (s.z, s.x), 0)
    for ky in range(s.slab_y):
        inverse = jnp.full((s.z, s.x), -1, jnp.int32)
        for c in range(s.c):
            lane = ky * s.c + c
            inverse = jnp.where(turned[lane : lane + 1, :] == cells, lane, inverse)
        inverse_ref[ky] = inverse.T
    wave_x = lax.broadcasted_iota(jnp.int32, depth.shape, 0)
    wave_y = part_ref[0] * s.slab_y + lane_numbers(depth.shape) // s.c
    kinetic = wave_energy(wave_x, s.x) + wave_energy(wave_y, s.y) + wave_energy(depth, s.z)
    diag_ref[...] = 1.0 / (kinetic - energy_ref[slot_ref[0]])
    send_lines(s, psi_ref[...], inverse_ref, tx_ref[...], send_ref)


def band_kernel(s, recv_ref, local_ref, tyl_ref, tzr_ref, image_ref, grid_ref):
    table_y, table_z = tyl_ref[...], tzr_ref[...]
    group = min(s.slab_x, GROUP)
    for first in range(0, s.slab_x, group):
        inner = slabs_in(s, recv_ref, range(first, first + group), table_y)
        rows = pl.ds(first * s.y, group * s.y)
        grid = from_right(inner, table_z)
        grid_ref[rows, :] = grid
        outer = from_right(local_ref[rows, :] * grid, table_z)
        slabs_out(s, outer, table_y, image_ref, range(first, first + group))


def driving_kernel(s, pert_ref, grid_ref, trial_ref, tyl_ref, tzr_ref, send_ref):
    table_y, table_z = tyl_ref[...], tzr_ref[...]
    group = min(s.slab_x, GROUP)
    for first in range(0, s.slab_x, group):
        rows = pl.ds(first * s.y, group * s.y)
        outer = from_right(trial_ref[pert_ref[0], rows, :] * grid_ref[rows, :], table_z)
        slabs_out(s, outer, table_y, send_ref, range(first, first + group))


def image_kernel(s, recv_ref, depth_ref, tx_ref, image_ref):
    image_ref[...] = read_lines(s, recv_ref, depth_ref[...], tx_ref[...])


def project_kernel(s, recv_ref, depth_ref, all_ref, tx_ref, driving_ref, dots_ref):
    driving = read_lines(s, recv_ref, depth_ref[...], tx_ref[...])
    driving_ref[...] = driving
    dots = fold(band_dots(all_ref, driving))
    dots_ref[...] = jnp.broadcast_to(dots[None], dots_ref.shape)


def first_kernel(s, coef_total, dots_ref, driving_ref, all_ref, diag_ref, inverse_ref,
                 tx_ref, send_ref, start_ref):
    weights = total_weights(dots_ref[...], coef_total)
    start = band_sum(all_ref, weights) - driving_ref[...]
    start_ref[...] = start
    send_lines(s, start * diag_ref[...], inverse_ref, tx_ref[...], send_ref)


def potential_kernel(s, dots_ref, *refs):
    dots = dots_ref[...]
    block = s.slab_x * s.slab_y
    apply_potential(s, *refs)
    refs[-1][:, block:, :] = jnp.broadcast_to(dots[None], (s.parts,) + dots.shape)


def apply_potential(s, recv_ref, local_ref, tyl_ref, tzr_ref, send_ref):
    table_y, table_z = tyl_ref[...], tzr_ref[...]
    group = min(s.slab_x, GROUP)
    for first in range(0, s.slab_x, group):
        inner = slabs_in(s, recv_ref, range(first, first + group), table_y)
        rows = pl.ds(first * s.y, group * s.y)
        grid = from_right(inner, table_z)
        outer = from_right(local_ref[rows, :] * grid, table_z)
        slabs_out(s, outer, table_y, send_ref, range(first, first + group))


def state_dots(bands, images, diag, state):
    return fold(band_dots(bands, state) + band_dots(images, diag * state))


def first_dots_kernel(s, held_ref, all_ref, image_ref, diag_ref, start_ref, send_ref):
    dots = state_dots(all_ref, image_ref, diag_ref[...], start_ref[...])
    block = s.slab_x * s.slab_y
    send_ref[:, block:, :] = jnp.broadcast_to(dots[None], (s.parts,) + dots.shape)


def update_kernel(s, coef_total, last, pert_ref, recv_ref, start_ref, depth_ref, all_ref,
                  image_ref, diag_ref, inverse_ref, tx_ref, own_ref, other_ref, send_ref, dots_ref=None):
    block = s.slab_x * s.slab_y
    table_x = tx_ref[...]
    weights = total_weights(recv_ref[:, block:, :], coef_total)
    change = read_lines(s, recv_ref, depth_ref[...], table_x)
    diag = diag_ref[...]
    state = start_ref[...] - change + band_sum(all_ref, weights)
    response = state * diag
    send_lines(s, response, inverse_ref, table_x, send_ref)
    if not last:
        dots_ref[...] = state_dots(all_ref, image_ref, diag, state)
        return
    own = jnp.sum(own_ref[...] * response, axis=0, keepdims=True)
    other = jnp.sum(other_ref[...] * response, axis=0, keepdims=True)
    lead = pert_ref[0] == 0
    rest = jnp.zeros((6, own.shape[1]), F32)
    sums = jnp.concatenate(
        [jnp.where(lead, own, other), jnp.where(lead, other, own), rest], axis=0
    )
    send_ref[:, block:, :] = jnp.broadcast_to(sums[None], (s.parts,) + sums.shape)


def density_kernel(s, bands, core_ref, recv_ref, grid_ref, tyl_ref, tzr_ref, send_ref):
    table_y, table_z = tyl_ref[...], tzr_ref[...]
    group = min(s.slab_x, GROUP)
    keep = s.y // bands
    for first in range(0, s.slab_x, group):
        inner = slabs_in(s, recv_ref, range(first, first + group), table_y)
        rows = pl.ds(first * s.y, group * s.y)
        density = 2.0 * grid_ref[rows, :] * from_right(inner, table_z)
        for row in range(group):
            for band in range(bands):
                start = row * s.y + band * keep
                place = (first + row) * keep
                slot = core_ref[0] if band % 2 == 0 else 1 - core_ref[0]
                send_ref[slot, band // 2, place : place + keep, :] = density[start : start + keep]
    sums = jnp.sum(recv_ref[:, s.slab_x * s.slab_y :, :], axis=0)
    send_ref[:, :, s.slab_x * keep :, :] = jnp.broadcast_to(
        sums[None, None], (2, bands // 2) + sums.shape
    )


def final_kernel(s, rows, recv_ref, density_ref, sums_ref):
    total = jnp.sum(recv_ref[...], axis=0)
    density_ref[...] = total[:rows]
    lanes = jnp.sum(total[rows:], axis=1, keepdims=True)
    sums_ref[...] = jnp.broadcast_to(lanes, sums_ref.shape)


def call(kernel, out_shape, scalars=0, name=None, aliases=None):
    smem = pl.BlockSpec(memory_space=pltpu.SMEM)
    vmem = pl.BlockSpec(memory_space=pltpu.VMEM)

    def run(*operands):
        return pl.pallas_call(
            kernel,
            out_shape=out_shape,
            in_specs=[smem] * scalars + [vmem] * (len(operands) - scalars),
            out_specs=jax.tree.map(lambda _: vmem, out_shape),
            compiler_params=pltpu.CompilerParams(vmem_limit_bytes=VMEM_LIMIT),
            input_output_aliases=aliases or {},
            name=name,
        )(*operands)

    return run


def shape(*sizes, dtype=F32):
    return jax.ShapeDtypeStruct(sizes, dtype)


def per_device(trial_potential, local_potential, psi_coef, band_energy, band_slot, pw_index):
    parts = lax.axis_size("pw")
    band_count = lax.axis_size("band")
    slab_x, size_y, size_z = local_potential.shape
    size_x = slab_x * parts
    coef_count = psi_coef.shape[0]
    coef_total = coef_count * parts
    total_bands = band_energy.shape[0]
    total_perts = trial_potential.shape[0]
    slab_y = size_y // parts
    s = Sizes(size_x, size_y, size_z, parts, coef_count // (size_x * slab_y))
    block = slab_x * slab_y
    flat = (size_x, slab_y * s.c)
    pert = lax.axis_index("pert").astype(jnp.int32)
    part = lax.axis_index("pw").astype(jnp.int32)
    core = lax.axis_index("band").astype(jnp.int32) & 1
    own_column = lax.broadcasted_iota(jnp.int32, (total_perts, total_perts), 1) == pert
    part, pert, core, own_column, slot = lax.optimization_barrier(
        (part.reshape(1), pert.reshape(1), core.reshape(1), own_column, band_slot)
    )

    table_x = jnp.asarray(left_table(size_x))
    table_y = jnp.asarray(left_table(size_y))
    table_z = jnp.asarray(right_table(size_z))

    def exchange(values):
        return lax.all_to_all(values, "pw", split_axis=0, concat_axis=0, tiled=True)

    psi = psi_coef.reshape(flat)
    index = pw_index.reshape(flat)
    all_psi = lax.all_gather(psi, "band", axis=0)
    anywhere = pl.BlockSpec(memory_space=pltpu.HBM)
    smem = pl.BlockSpec(memory_space=pltpu.SMEM)
    vmem = pl.BlockSpec(memory_space=pltpu.VMEM)
    send, inverse, depth, diag = pl.pallas_call(
        partial(start_kernel, s),
        out_shape=(
            shape(parts, block, size_z),
            shape(slab_y, size_x, size_z, dtype=jnp.int32),
            shape(*flat, dtype=jnp.int32),
            shape(*flat),
        ),
        in_specs=[smem, smem] + [anywhere] * 4,
        out_specs=(vmem,) * 4,
        scratch_shapes=[
            pltpu.SMEM(band_energy.shape, F32),
            pltpu.VMEM(flat, F32),
            pltpu.VMEM(flat, jnp.int32),
            pltpu.VMEM(table_x.shape, BF16),
            pltpu.SemaphoreType.DMA((4,)),
        ],
        compiler_params=pltpu.CompilerParams(vmem_limit_bytes=VMEM_LIMIT),
        name="start",
    )(part, slot, band_energy, psi, index, table_x)
    recv = exchange(send)

    local = local_potential.reshape(slab_x * size_y, size_z)
    trials = trial_potential.reshape(total_perts, slab_x * size_y, size_z)
    send, psi_grid = call(
        partial(band_kernel, s),
        (shape(parts, block, size_z), shape(slab_x * size_y, size_z)),
        0,
        "band",
    )(recv, local, table_y, table_z)
    recv = exchange(send)
    image = call(partial(image_kernel, s), shape(*flat), 0, "image")(recv, depth, table_x)
    all_image = lax.all_gather(image, "band", axis=0)
    psi_grid, image = lax.optimization_barrier((psi_grid, image))
    send = call(partial(driving_kernel, s), shape(parts, block, size_z), 1, "driving")(
        pert, psi_grid, trials, table_y, table_z
    )
    recv = exchange(send)
    driving, dots = call(
        partial(project_kernel, s),
        (shape(*flat), shape(parts, total_bands // 2, size_z)),
        0,
        "project",
    )(recv, depth, all_psi, table_x)
    dots = exchange(dots)
    send, start = call(
        partial(first_kernel, s, coef_total),
        (shape(parts, block, size_z), shape(*flat)),
        0,
        "first",
    )(dots, driving, all_psi, diag, inverse, table_x)
    for iteration in range(ITERS):
        last = iteration == ITERS - 1
        recv = exchange(send)
        out = shape(parts, block + total_bands // 2, size_z)
        if iteration == 0:
            send = call(partial(apply_potential, s), out, 0, "potential")(
                recv, local, table_y, table_z
            )
            send, driving = lax.optimization_barrier((send, driving))
            other = lax.ppermute(driving, "pert", [(0, 1), (1, 0)])
            send, all_image, other = lax.optimization_barrier((send, all_image, other))
            send = call(partial(first_dots_kernel, s), out, 0, "dots", {0: 0})(
                send, all_psi, all_image, diag, start
            )
        else:
            send = call(partial(potential_kernel, s), out, 0, "potential")(
                dots, recv, local, table_y, table_z
            )
        recv = exchange(send)
        if last:
            outs = (shape(parts, block + 8, size_z),)
        else:
            outs = (shape(parts, block, size_z), shape(total_bands // 2, size_z))
        send, *rest = call(partial(update_kernel, s, coef_total, last), outs, 1, "update")(
            pert, recv, start, depth, all_psi, all_image, diag, inverse, table_x, driving,
            other,
        )
        dots = rest[0] if rest else None

    recv = exchange(send)
    rows = slab_x * (size_y // band_count)
    send = call(
        partial(density_kernel, s, band_count),
        shape(2, band_count // 2, rows + 8, size_z),
        1,
        "density",
    )(core, recv, psi_grid, table_y, table_z)
    got = lax.ppermute(send[1], "band", [(band, band ^ 1) for band in range(band_count)])
    near = [[2 * z + c for z in range(band_count // 2)] for c in range(2)]
    recv = lax.all_to_all(
        send[0] + got, "band", split_axis=0, concat_axis=0, tiled=True, axis_index_groups=near
    )
    density, sums = call(
        partial(final_kernel, s, rows), (shape(rows, size_z), shape(8, size_z)), 0, "final"
    )(recv)
    own = sums[:total_perts, :total_perts] * (2.0 / (total_bands * coef_total))
    across = lax.ppermute(own, "pert", [(0, 1), (1, 0)])
    intersections = jnp.where(own_column, own, across)
    return (
        density.reshape(1, slab_x, size_y // band_count, size_z),
        intersections,
    )


def solution(mesh):
    return jax.shard_map(
        per_device,
        mesh=mesh,
        in_specs=(
            P(None, "pw", None, None),
            P("pw", None, None),
            P("pw", "band"),
            P(),
            P("band"),
            P("pw"),
        ),
        out_specs=(P("pert", "pw", "band", None), P()),
        check_vma=False,
    )
```

profile of v0, /device:TPU:2, one launch (start us, length us, event | category | flops | bytes accessed | tf_op | source)
XLA Modules:
  0.0 213.4 jit_solution(12765884424828202226)
XLA Ops:
  11.0 2.2 %start.1 = (f32[8,128,128]{2,1,0:T(8,128)S(1)}, s32[8,128,128]{2,1,0:T(8,128)S(1)}, s32[128,128]{1,0:T(8,128)S(1)}, f32[128,128]{1,0:T(8,128)S(1)}) custom-call(s32[1]{0:T(128)} %bitcast.part_ref, s32[1]{0:T(128)S(6)} %copy.13.slot_ref, f32[16]{0:T(128)S(1)} %copy-done.18, f32[128,128]{1,0:T(8,128)S(1)} %bitcast.26, s32[128,128]{1,0:T(8,128)S(1)} %bitcast.27, ...), custom_call_target="tpu_custom_call" | custom-call | tf_op jit(solution)/shard_map/start/pallas_call | solution.py:361
  13.2 17.5 %all_to_all.60.recv_ref = f32[8,128,128]{2,1,0:T(8,128)S(1)} all-to-all(f32[8,128,128]{2,1,0:T(8,128)S(1)} %get-tuple-element.33), channel_id=1, replica_groups=mesh['pert'=2,'band'=16,'pw'=8] {'pw'}, dimensions={0} | all-to-all | bytes 1048576 | tf_op jit(solution)/shard_map/all_to_all | solution.py:353
  31.6 13.1 %all_to_all.61.recv_ref = f32[8,128,128]{2,1,0:T(8,128)S(1)} all-to-all(f32[8,128,128]{2,1,0:T(8,128)S(1)} %get-tuple-element.35), channel_id=1, replica_groups=mesh['pert'=2,'band'=16,'pw'=8] {'pw'}, dimensions={0} | all-to-all | bytes 1048576 | tf_op jit(solution)/shard_map/all_to_all | solution.py:353
  44.6 1.2 image.1
  46.5 12.7 %all_to_all.62.recv_ref = f32[8,128,128]{2,1,0:T(8,128)S(1)} all-to-all(f32[8,128,128]{2,1,0:T(8,128)S(1)} %driving.1), channel_id=1, replica_groups=mesh['pert'=2,'band'=16,'pw'=8] {'pw'}, dimensions={0} | all-to-all | bytes 1048576 | tf_op jit(solution)/shard_map/all_to_all | solution.py:353
  59.2 1.2 copy-done
  61.1 10.3 %all_to_all.63.dots_ref = f32[8,8,128]{2,1,0:T(8,128)S(1)} all-to-all(f32[8,8,128]{2,1,0:T(8,128)S(1)} %get-tuple-element.38), channel_id=1, replica_groups=mesh['pert'=2,'band'=16,'pw'=8] {'pw'}, dimensions={0} | all-to-all | bytes 65536 | tf_op jit(solution)/shard_map/all_to_all | solution.py:353
  72.9 13.2 %all_to_all.64.recv_ref = f32[8,128,128]{2,1,0:T(8,128)S(1)} all-to-all(f32[8,128,128]{2,1,0:T(8,128)S(1)} %get-tuple-element.42), channel_id=1, replica_groups=mesh['pert'=2,'band'=16,'pw'=8] {'pw'}, dimensions={0} | all-to-all | bytes 1048576 | tf_op jit(solution)/shard_map/all_to_all | solution.py:353
  87.0 1.5 collective-permute-start
  88.5 2.9 %collective-permute-done.other_ref = f32[128,128]{1,0:T(8,128)S(1)} collective-permute-done((f32[128,128]{1,0:T(8,128)S(1)}, f32[128,128]{1,0:T(8,128)S(1)}, u32[]{:S(2)}, u32[]{:S(2)}) %collective-permute-start) | collective-permute-done | bytes 65568 | tf_op jit(solution)/shard_map/ppermute | solution.py:421
  92.0 1.2 copy-done.2
  94.3 16.8 %all_to_all.65.recv_ref = f32[8,136,128]{2,1,0:T(8,128)S(1)} all-to-all(f32[8,136,128]{2,1,0:T(8,128)S(1)} %dots.1), channel_id=1, replica_groups=mesh['pert'=2,'band'=16,'pw'=8] {'pw'}, dimensions={0} | all-to-all | bytes 1114112 | tf_op jit(solution)/shard_map/all_to_all | solution.py:353
  111.2 1.3 update.3
  112.4 13.8 %all_to_all.66.refs_0_ = f32[8,128,128]{2,1,0:T(8,128)S(1)} all-to-all(f32[8,128,128]{2,1,0:T(8,128)S(1)} %get-tuple-element.50), channel_id=1, replica_groups=mesh['pert'=2,'band'=16,'pw'=8] {'pw'}, dimensions={0} | all-to-all | bytes 1048576 | tf_op jit(solution)/shard_map/all_to_all | solution.py:353
  127.1 13.4 %all_to_all.67.recv_ref = f32[8,136,128]{2,1,0:T(8,128)S(1)} all-to-all(f32[8,136,128]{2,1,0:T(8,128)S(1)} %potential.4), channel_id=1, replica_groups=mesh['pert'=2,'band'=16,'pw'=8] {'pw'}, dimensions={0} | all-to-all | bytes 1114112 | tf_op jit(solution)/shard_map/all_to_all | solution.py:353
  140.5 1.3 update.4
  141.8 12.5 %all_to_all.68.refs_0_ = f32[8,128,128]{2,1,0:T(8,128)S(1)} all-to-all(f32[8,128,128]{2,1,0:T(8,128)S(1)} %get-tuple-element.52), channel_id=1, replica_groups=mesh['pert'=2,'band'=16,'pw'=8] {'pw'}, dimensions={0} | all-to-all | bytes 1048576 | tf_op jit(solution)/shard_map/all_to_all | solution.py:353
  155.2 13.1 %all_to_all.69.recv_ref = f32[8,136,128]{2,1,0:T(8,128)S(1)} all-to-all(f32[8,136,128]{2,1,0:T(8,128)S(1)} %potential.5), channel_id=1, replica_groups=mesh['pert'=2,'band'=16,'pw'=8] {'pw'}, dimensions={0} | all-to-all | bytes 1114112 | tf_op jit(solution)/shard_map/all_to_all | solution.py:353
  168.3 1.2 update.5
  169.6 13.0 %all_to_all.70.recv_ref = f32[8,136,128]{2,1,0:T(8,128)S(1)} all-to-all(f32[8,136,128]{2,1,0:T(8,128)S(1)} %update.5), channel_id=1, replica_groups=mesh['pert'=2,'band'=16,'pw'=8] {'pw'}, dimensions={0} | all-to-all | bytes 1114112 | tf_op jit(solution)/shard_map/all_to_all | solution.py:353
  183.3 1.6 collective-permute-done.1
  184.9 16.9 %all_to_all.71.recv_ref = f32[8,72,128]{2,1,0:T(8,128)S(1)} all-to-all(f32[8,72,128]{2,1,0:T(8,128)S(1)} %fusion), channel_id=1, replica_groups={{0,16,32,48,64,80,96,112},{8,24,40,56,72,88,104,120},{1,17,33,49,65,81,..., dimensions={0} | all-to-all | bytes 589824 | tf_op jit(solution)/shard_map/all_to_all | solution.py:451
  202.4 1.4 collective-permute-start.2
  203.8 2.1 %collective-permute-done.2 = f32[2,2]{1,0:T(2,128)S(1)} collective-permute-done((f32[2,2]{1,0:T(2,128)S(1)}, f32[2,2]{1,0:T(2,128)S(1)}, u32[]{:S(2)}, u32[]{:S(2)}) %collective-permute-start.2) | collective-permute-done | bytes 48 | tf_op jit(solution)/shard_map/ppermute | solution.py:458
  (59 shorter events, 13.0 us)
Async XLA Ops:
  7.2 1.5 copy-start.5
  7.2 52.0 %all-gather.4.cloned.1.call-start = ((), (), s32[]{:S(2)}) async-start(), calls=%async_computation.12 | async-start | bytes 1114112 | tf_op jit(solution)/shard_map/all_gather | solution.py:357
  7.9 84.1 %all-gather.6.cloned.1.call-start = ((), (), s32[]{:S(2)}) async-start(), calls=%async_computation.13 | async-start | bytes 1114112 | tf_op jit(solution)/shard_map/all_gather | solution.py:393
  8.6 0.7 copy-start.18
  9.3 0.8 copy-start.16
  10.1 0.8 copy-start.17
  13.2 17.5 %copy-start.4 = (f32[16,64,128]{2,1,0:T(8,128)S(1)}, f32[16,64,128]{2,1,0:T(8,128)}, u32[]{:S(2)}) copy-start(f32[16,64,128]{2,1,0:T(8,128)} %param.10) | copy-start | bytes 1572868
  13.2 17.5 %copy-start.6 = (bf16[384,128]{1,0:T(8,128)(2,1)S(1)}, bf16[384,128]{1,0:T(8,128)(2,1)}, u32[]{:S(2)}) copy-start(bf16[384,128]{1,0:T(8,128)(2,1)} %constant.26.clone.tzr_ref.refs_3_) | copy-start | bytes 294916
  13.2 17.5 %copy-start.7 = (bf16[64,192]{1,0:T(8,128)(2,1)S(1)}, bf16[64,192]{1,0:T(8,128)(2,1)}, u32[]{:S(2)}) copy-start(bf16[64,192]{1,0:T(8,128)(2,1)} %constant.25.clone.tyl_ref.refs_2_) | copy-start | bytes 73732
  31.6 14.3 %copy-start.13 = (f32[2,16,64,128]{3,2,1,0:T(8,128)S(1)}, f32[2,16,64,128]{3,2,1,0:T(8,128)}, u32[]{:S(2)}) copy-start(f32[2,16,64,128]{3,2,1,0:T(8,128)} %param.9) | copy-start | bytes 3145732
  59.2 1.2 copy-start
  61.1 25.9 %copy-start.8 = (f32[128,128]{1,0:T(8,128)}, f32[128,128]{1,0:T(8,128)S(1)}, u32[]{:S(2)}) copy-start(f32[128,128]{1,0:T(8,128)S(1)} %get-tuple-element.44.driving_ref.own_ref) | copy-start | bytes 196612
  72.3 0.6 copy-start.10
  86.1 5.9 %copy-start.1 = (f32[16,128,128]{2,1,0:T(8,128)S(1)}, f32[16,128,128]{2,1,0:T(8,128)}, u32[]{:S(2)}) copy-start(f32[16,128,128]{2,1,0:T(8,128)} %all-gather.4.cloned.1.call-done.all_ref) | copy-start | bytes 3145732
  87.0 4.4 %collective-permute-start = (f32[128,128]{1,0:T(8,128)S(1)}, f32[128,128]{1,0:T(8,128)S(1)}, u32[]{:S(2)}, u32[]{:S(2)}) collective-permute-start(f32[128,128]{1,0:T(8,128)S(1)} %get-tuple-element.44.driving_ref.own_ref), channel_id=1, source_target_pairs={{0,128},{128,0},{1,129},{129,1},{2,130},{130,2},{3,131},{131,3},{4... | collective-permute-start | bytes 196616 | tf_op jit(solution)/shard_map/ppermute | solution.py:421
  91.4 0.6 copy-start.14
  92.0 1.2 copy-start.2
  93.2 0.8 copy-start.11
  94.0 17.1 %copy-start.12 = (f32[128,128]{1,0:T(8,128)S(1)}, f32[128,128]{1,0:T(8,128)}, u32[]{:S(2)}) copy-start(f32[128,128]{1,0:T(8,128)} %copy-done.10) | copy-start | bytes 196612
  94.1 17.1 %copy-start.15 = (f32[128,128]{1,0:T(8,128)S(1)}, f32[128,128]{1,0:T(8,128)}, u32[]{:S(2)}) copy-start(f32[128,128]{1,0:T(8,128)} %copy-done.14) | copy-start | bytes 196612
  94.3 16.9 %copy-start.3 = (f32[2048,128]{1,0:T(8,128)S(1)}, f32[2048,128]{1,0:T(8,128)}, u32[]{:S(2)}) copy-start(f32[2048,128]{1,0:T(8,128)} %all-gather.6.cloned.1.call-done) | copy-start | bytes 3145732
  94.3 16.9 %copy-start.9 = (f32[128,128]{1,0:T(8,128)S(1)}, f32[128,128]{1,0:T(8,128)}, u32[]{:S(2)}) copy-start(f32[128,128]{1,0:T(8,128)} %copy-done.8) | copy-start | bytes 196612
  183.2 1.7 collective-permute-start.1
  202.4 3.6 %collective-permute-start.2 = (f32[2,2]{1,0:T(2,128)S(1)}, f32[2,2]{1,0:T(2,128)S(1)}, u32[]{:S(2)}, u32[]{:S(2)}) collective-permute-start(f32[2,2]{1,0:T(2,128)S(1)} %slice_multiply_fusion), channel_id=1, source_target_pairs={{0,128},{128,0},{1,129},{129,1},{2,130},{130,2},{3,131},{131,3},{4... | collective-permute-start | bytes 56 | tf_op jit(solution)/shard_map/ppermute | solution.py:458
Sparse Core Ops, SparseCore 0:
  9.8 41.4 all-gather.3
  53.1 37.2 all-gather.5
where the time goes:
time: 214 us; the launch traced here: 213 us
  blocking collectives  166 us (78%)
  between operations  14.9 us (7%)
  Pallas kernels  14.1 us (7%)
  waiting for transfers between devices  7.31 us (3%)
  local copies, waits for them, and re-layouts  6.94 us (3%)
  starting transfers between devices  3.05 us (1%)
    all_to_all x11, blocking collectives, exchange(): return lax.all_to_all(values, 'pw', split_axis=0, concat_axis=0, tiled=True)  150 us
    all_to_all x1, blocking collectives, per_device(): lax.all_to_all(send[0] + got, 'band', split_axis=0, concat_axis=0, tiled=...  16.9 us
    pallas_call x14, Pallas kernels, run(): pl.pallas_call(kernel, out_shape=out_shape, in_specs=[smem] * scalars + [...  11.9 us
    unnamed x38, local copies, waits for them, and re-layouts  6.91 us
  transfers between devices with their start and end apart: 5, of which 3 were waited for; matrix products, arithmetic and copies ran while one was open for 0% of the time, Pallas kernels for 3%

commit v1 on v0

--- a/solution.py
+++ b/solution.py
@@ -246,6 +246,12 @@
     return fold(band_dots(bands, state) + band_dots(images, diag * state))
 
 
+def first_potential_kernel(s, start_ref, recv_ref, local_ref, tyl_ref, tzr_ref, send_ref,
+                           kept_ref):
+    kept_ref[...] = start_ref[...]
+    apply_potential(s, recv_ref, local_ref, tyl_ref, tzr_ref, send_ref)
+
+
 def first_dots_kernel(s, held_ref, all_ref, image_ref, diag_ref, start_ref, send_ref):
     dots = state_dots(all_ref, image_ref, diag_ref[...], start_ref[...])
     block = s.slab_x * s.slab_y
@@ -414,14 +420,14 @@
         recv = exchange(send)
         out = shape(parts, block + total_bands // 2, size_z)
         if iteration == 0:
-            send = call(partial(apply_potential, s), out, 0, "potential")(
-                recv, local, table_y, table_z
-            )
+            send, kept = call(
+                partial(first_potential_kernel, s), (out, shape(*flat)), 0, "potential"
+            )(start, recv, local, table_y, table_z)
             send, driving = lax.optimization_barrier((send, driving))
             other = lax.ppermute(driving, "pert", [(0, 1), (1, 0)])
             send, all_image, other = lax.optimization_barrier((send, all_image, other))
             send = call(partial(first_dots_kernel, s), out, 0, "dots", {0: 0})(
-                send, all_psi, all_image, diag, start
+                send, all_psi, all_image, diag, kept
             )
         else:
             send = call(partial(potential_kernel, s), out, 0, "potential")(

time: 214 us -> 214 us (level)
    unnamed x38 -> x40, local copies, waits for them, and re-layouts: 6.91 us -> 6.89 us
where the time goes in v1:
time: 214 us; the launch traced here: 213 us
  blocking collectives  167 us (78%)
  between operations  14.9 us (7%)
  Pallas kernels  14.1 us (7%)
  waiting for transfers between devices  7.6 us (4%)
  local copies, waits for them, and re-layouts  6.92 us (3%)
  starting transfers between devices  2.67 us (1%)
    all_to_all x11, blocking collectives, exchange(): return lax.all_to_all(values, 'pw', split_axis=0, concat_axis=0, tiled=True)  150 us
    all_to_all x1, blocking collectives, per_device(): lax.all_to_all(send[0] + got, 'band', split_axis=0, concat_axis=0, tiled=...  16.9 us
    pallas_call x14, Pallas kernels, run(): pl.pallas_call(kernel, out_shape=out_shape, in_specs=[smem] * scalars + [...  12 us
    unnamed x40, local copies, waits for them, and re-layouts  6.89 us
  transfers between devices with their start and end apart: 5, of which 3 were waited for; matrix products, arithmetic and copies ran while one was open for 0% of the time, Pallas kernels for 3%

profile of v1, /device:TPU:2, one launch (start us, length us, event | category | flops | bytes accessed | tf_op | source)
XLA Modules:
  0.0 213.4 jit_solution(18208994071579112796)
XLA Ops:
  11.0 2.2 %start.1 = (f32[8,128,128]{2,1,0:T(8,128)S(1)}, s32[8,128,128]{2,1,0:T(8,128)S(1)}, s32[128,128]{1,0:T(8,128)S(1)}, f32[128,128]{1,0:T(8,128)S(1)}) custom-call(s32[1]{0:T(128)} %bitcast.part_ref, s32[1]{0:T(128)S(6)} %copy.13.slot_ref, f32[16]{0:T(128)S(1)} %copy-done.19, f32[128,128]{1,0:T(8,128)S(1)} %bitcast.26, s32[128,128]{1,0:T(8,128)S(1)} %bitcast.27, ...), custom_call_target="tpu_custom_call" | custom-call | tf_op jit(solution)/shard_map/start/pallas_call | solution.py:367
  13.2 17.5 %all_to_all.60.recv_ref = f32[8,128,128]{2,1,0:T(8,128)S(1)} all-to-all(f32[8,128,128]{2,1,0:T(8,128)S(1)} %get-tuple-element.35), channel_id=1, replica_groups=mesh['pert'=2,'band'=16,'pw'=8] {'pw'}, dimensions={0} | all-to-all | bytes 1048576 | tf_op jit(solution)/shard_map/all_to_all | solution.py:359
  31.6 13.1 %all_to_all.61.recv_ref = f32[8,128,128]{2,1,0:T(8,128)S(1)} all-to-all(f32[8,128,128]{2,1,0:T(8,128)S(1)} %get-tuple-element.37), channel_id=1, replica_groups=mesh['pert'=2,'band'=16,'pw'=8] {'pw'}, dimensions={0} | all-to-all | bytes 1048576 | tf_op jit(solution)/shard_map/all_to_all | solution.py:359
  44.6 1.2 image.1
  46.5 12.7 %all_to_all.62.recv_ref = f32[8,128,128]{2,1,0:T(8,128)S(1)} all-to-all(f32[8,128,128]{2,1,0:T(8,128)S(1)} %driving.1), channel_id=1, replica_groups=mesh['pert'=2,'band'=16,'pw'=8] {'pw'}, dimensions={0} | all-to-all | bytes 1048576 | tf_op jit(solution)/shard_map/all_to_all | solution.py:359
  59.2 1.2 copy-done
  61.1 10.3 %all_to_all.63.dots_ref = f32[8,8,128]{2,1,0:T(8,128)S(1)} all-to-all(f32[8,8,128]{2,1,0:T(8,128)S(1)} %get-tuple-element.40), channel_id=1, replica_groups=mesh['pert'=2,'band'=16,'pw'=8] {'pw'}, dimensions={0} | all-to-all | bytes 65536 | tf_op jit(solution)/shard_map/all_to_all | solution.py:359
  72.3 13.4 %all_to_all.64.recv_ref = f32[8,128,128]{2,1,0:T(8,128)S(1)} all-to-all(f32[8,128,128]{2,1,0:T(8,128)S(1)} %get-tuple-element.45), channel_id=1, replica_groups=mesh['pert'=2,'band'=16,'pw'=8] {'pw'}, dimensions={0} | all-to-all | bytes 1048576 | tf_op jit(solution)/shard_map/all_to_all | solution.py:359
  87.2 1.1 collective-permute-start
  88.2 3.2 %collective-permute-done.other_ref = f32[128,128]{1,0:T(8,128)S(1)} collective-permute-done((f32[128,128]{1,0:T(8,128)S(1)}, f32[128,128]{1,0:T(8,128)S(1)}, u32[]{:S(2)}, u32[]{:S(2)}) %collective-permute-start) | collective-permute-done | bytes 65568 | tf_op jit(solution)/shard_map/ppermute | solution.py:427
  92.0 1.2 copy-done.2
  94.4 16.8 %all_to_all.65.recv_ref = f32[8,136,128]{2,1,0:T(8,128)S(1)} all-to-all(f32[8,136,128]{2,1,0:T(8,128)S(1)} %dots.1), channel_id=1, replica_groups=mesh['pert'=2,'band'=16,'pw'=8] {'pw'}, dimensions={0} | all-to-all | bytes 1114112 | tf_op jit(solution)/shard_map/all_to_all | solution.py:359
  111.2 1.3 update.3
  112.4 13.8 %all_to_all.66.refs_0_ = f32[8,128,128]{2,1,0:T(8,128)S(1)} all-to-all(f32[8,128,128]{2,1,0:T(8,128)S(1)} %get-tuple-element.54), channel_id=1, replica_groups=mesh['pert'=2,'band'=16,'pw'=8] {'pw'}, dimensions={0} | all-to-all | bytes 1048576 | tf_op jit(solution)/shard_map/all_to_all | solution.py:359
  127.1 13.4 %all_to_all.67.recv_ref = f32[8,136,128]{2,1,0:T(8,128)S(1)} all-to-all(f32[8,136,128]{2,1,0:T(8,128)S(1)} %potential.4), channel_id=1, replica_groups=mesh['pert'=2,'band'=16,'pw'=8] {'pw'}, dimensions={0} | all-to-all | bytes 1114112 | tf_op jit(solution)/shard_map/all_to_all | solution.py:359
  140.5 1.3 update.4
  141.8 12.5 %all_to_all.68.refs_0_ = f32[8,128,128]{2,1,0:T(8,128)S(1)} all-to-all(f32[8,128,128]{2,1,0:T(8,128)S(1)} %get-tuple-element.56), channel_id=1, replica_groups=mesh['pert'=2,'band'=16,'pw'=8] {'pw'}, dimensions={0} | all-to-all | bytes 1048576 | tf_op jit(solution)/shard_map/all_to_all | solution.py:359
  155.2 13.2 %all_to_all.69.recv_ref = f32[8,136,128]{2,1,0:T(8,128)S(1)} all-to-all(f32[8,136,128]{2,1,0:T(8,128)S(1)} %potential.5), channel_id=1, replica_groups=mesh['pert'=2,'band'=16,'pw'=8] {'pw'}, dimensions={0} | all-to-all | bytes 1114112 | tf_op jit(solution)/shard_map/all_to_all | solution.py:359
  168.4 1.2 update.5
  169.6 13.0 %all_to_all.70.recv_ref = f32[8,136,128]{2,1,0:T(8,128)S(1)} all-to-all(f32[8,136,128]{2,1,0:T(8,128)S(1)} %update.5), channel_id=1, replica_groups=mesh['pert'=2,'band'=16,'pw'=8] {'pw'}, dimensions={0} | all-to-all | bytes 1114112 | tf_op jit(solution)/shard_map/all_to_all | solution.py:359
  183.3 1.6 collective-permute-done.1
  184.9 16.9 %all_to_all.71.recv_ref = f32[8,72,128]{2,1,0:T(8,128)S(1)} all-to-all(f32[8,72,128]{2,1,0:T(8,128)S(1)} %fusion), channel_id=1, replica_groups={{0,16,32,48,64,80,96,112},{8,24,40,56,72,88,104,120},{1,17,33,49,65,81,..., dimensions={0} | all-to-all | bytes 589824 | tf_op jit(solution)/shard_map/all_to_all | solution.py:457
  202.4 1.4 collective-permute-start.2
  203.8 2.1 %collective-permute-done.2 = f32[2,2]{1,0:T(2,128)S(1)} collective-permute-done((f32[2,2]{1,0:T(2,128)S(1)}, f32[2,2]{1,0:T(2,128)S(1)}, u32[]{:S(2)}, u32[]{:S(2)}) %collective-permute-start.2) | collective-permute-done | bytes 48 | tf_op jit(solution)/shard_map/ppermute | solution.py:464
  (61 shorter events, 12.9 us)
Async XLA Ops:
  7.2 1.5 copy-start.5
  7.2 52.0 %all-gather.4.cloned.1.call-start = ((), (), s32[]{:S(2)}) async-start(), calls=%async_computation.12 | async-start | bytes 1114112 | tf_op jit(solution)/shard_map/all_gather | solution.py:363
  7.9 84.1 %all-gather.6.cloned.1.call-start = ((), (), s32[]{:S(2)}) async-start(), calls=%async_computation.13 | async-start | bytes 1114112 | tf_op jit(solution)/shard_map/all_gather | solution.py:399
  8.6 0.7 copy-start.19
  9.3 0.8 copy-start.15
  10.1 0.8 copy-start.16
  13.2 17.5 %copy-start.4 = (f32[16,64,128]{2,1,0:T(8,128)S(1)}, f32[16,64,128]{2,1,0:T(8,128)}, u32[]{:S(2)}) copy-start(f32[16,64,128]{2,1,0:T(8,128)} %param.10) | copy-start | bytes 1572868
  13.2 17.5 %copy-start.6 = (bf16[384,128]{1,0:T(8,128)(2,1)S(1)}, bf16[384,128]{1,0:T(8,128)(2,1)}, u32[]{:S(2)}) copy-start(bf16[384,128]{1,0:T(8,128)(2,1)} %constant.26.clone.tzr_ref.refs_3_) | copy-start | bytes 294916
  13.2 17.5 %copy-start.7 = (bf16[64,192]{1,0:T(8,128)(2,1)S(1)}, bf16[64,192]{1,0:T(8,128)(2,1)}, u32[]{:S(2)}) copy-start(bf16[64,192]{1,0:T(8,128)(2,1)} %constant.25.clone.tyl_ref.refs_2_) | copy-start | bytes 73732
  31.6 14.3 %copy-start.12 = (f32[2,16,64,128]{3,2,1,0:T(8,128)S(1)}, f32[2,16,64,128]{3,2,1,0:T(8,128)}, u32[]{:S(2)}) copy-start(f32[2,16,64,128]{3,2,1,0:T(8,128)} %param.9) | copy-start | bytes 3145732
  59.2 1.2 copy-start
  61.1 26.1 %copy-start.8 = (f32[128,128]{1,0:T(8,128)}, f32[128,128]{1,0:T(8,128)S(1)}, u32[]{:S(2)}) copy-start(f32[128,128]{1,0:T(8,128)S(1)} %get-tuple-element.48.driving_ref.own_ref) | copy-start | bytes 196612
  72.3 13.4 %copy-start.10 = (f32[128,128]{1,0:T(8,128)}, f32[128,128]{1,0:T(8,128)S(1)}, u32[]{:S(2)}) copy-start(f32[128,128]{1,0:T(8,128)S(1)} %get-tuple-element.44.start_ref) | copy-start | bytes 196612
  72.3 19.8 %copy-start.1 = (f32[16,128,128]{2,1,0:T(8,128)S(1)}, f32[16,128,128]{2,1,0:T(8,128)}, u32[]{:S(2)}) copy-start(f32[16,128,128]{2,1,0:T(8,128)} %all-gather.4.cloned.1.call-done.all_ref) | copy-start | bytes 3145732
  87.2 4.3 %collective-permute-start = (f32[128,128]{1,0:T(8,128)S(1)}, f32[128,128]{1,0:T(8,128)S(1)}, u32[]{:S(2)}, u32[]{:S(2)}) collective-permute-start(f32[128,128]{1,0:T(8,128)S(1)} %get-tuple-element.48.driving_ref.own_ref), channel_id=1, source_target_pairs={{0,128},{128,0},{1,129},{129,1},{2,130},{130,2},{3,131},{131,3},{4... | collective-permute-start | bytes 196616 | tf_op jit(solution)/shard_map/ppermute | solution.py:427
  91.4 0.6 copy-start.13
  92.0 1.2 copy-start.2
  93.3 0.8 copy-start.18
  94.1 17.0 %copy-start.11 = (f32[128,128]{1,0:T(8,128)S(1)}, f32[128,128]{1,0:T(8,128)}, u32[]{:S(2)}) copy-start(f32[128,128]{1,0:T(8,128)} %copy-done.10) | copy-start | bytes 196612
  94.1 17.0 %copy-start.14 = (f32[128,128]{1,0:T(8,128)S(1)}, f32[128,128]{1,0:T(8,128)}, u32[]{:S(2)}) copy-start(f32[128,128]{1,0:T(8,128)} %copy-done.13) | copy-start | bytes 196612
  94.4 16.8 %copy-start.3 = (f32[2048,128]{1,0:T(8,128)S(1)}, f32[2048,128]{1,0:T(8,128)}, u32[]{:S(2)}) copy-start(f32[2048,128]{1,0:T(8,128)} %all-gather.6.cloned.1.call-done) | copy-start | bytes 3145732
  94.4 16.8 %copy-start.9 = (f32[128,128]{1,0:T(8,128)S(1)}, f32[128,128]{1,0:T(8,128)}, u32[]{:S(2)}) copy-start(f32[128,128]{1,0:T(8,128)} %copy-done.8) | copy-start | bytes 196612
  183.2 1.7 collective-permute-start.1
  202.4 3.6 %collective-permute-start.2 = (f32[2,2]{1,0:T(2,128)S(1)}, f32[2,2]{1,0:T(2,128)S(1)}, u32[]{:S(2)}, u32[]{:S(2)}) collective-permute-start(f32[2,2]{1,0:T(2,128)S(1)} %slice_multiply_fusion), channel_id=1, source_target_pairs={{0,128},{128,0},{1,129},{129,1},{2,130},{130,2},{3,131},{131,3},{4... | collective-permute-start | bytes 56 | tf_op jit(solution)/shard_map/ppermute | solution.py:464
  (1 other events, 0.6 us)
Sparse Core Ops, SparseCore 0:
  9.8 41.4 all-gather.3
  53.1 37.2 all-gather.5
